TPU v7x, 512 devices: a whole 4x4x16 slice. The times are simulated.
512 devices in a mesh: beam: 32 (over x_hi, z), band: 16 (over x_lo, y, core).
Axes of the slice: x: 4 (x_hi: 2, x_lo: 2; x = x_hi * 2 + x_lo), y: 4, z: 16, core: 2. Of those that a mesh axis runs over, the one named last changes fastest.
Arguments:
- intensity: bfloat16 [1280, 32, 4096], P('beam', None, 'band'), may hold values from -6 to 6
- chan_shift: int32 [32, 4096], P(None, 'band'), may hold values from 0 to 1
- sub_shift: int32 [1024, 256], replicated, may hold values from 0 to 5
- widths: int32 [16], replicated, may hold values from 1 to 128, as said below
Outputs:
- dm_series: bfloat16 [1024, 32, 512], P('band', 'beam')
- snr_peak: float32 [32, 16, 4], P('beam')
Inputs may be any that keep to these rules, and one draw needn't show every extreme that they name: `widths`: one boxcar has 128 samples and one has 1.
All inputs are finite; a program needn't handle non-finite values.
Results may differ from a plain program's by a relative error of at most 0.005.
Values may be sent and summed in bfloat16 or wider, within the bound.
A program may use at most 64 MiB of HBM per device.

v0:
```python
import math

import jax
import jax.numpy as jnp
from jax import lax
from jax.sharding import PartitionSpec as P

CHANNELS = 4096
CHSUB = 16
DMG = 32
TILE = 128
OUT_TILES = 4
CH_SHIFTS = 2
SUB_SHIFTS = 6
DMS = 1024
TIME = 512
MID_TILES = 9
TIME_IN = 1280


EPSILON = 1e-05


def dedisperse(series, shift_rows):
    group_count = series.shape[1]
    per_group = shift_rows.shape[0] // group_count
    shift_table = shift_rows.reshape(group_count, per_group, shift_rows.shape[1])
    summed = jnp.zeros((group_count, per_group, series.shape[0], TIME), jnp.float32)
    for offset in range(SUB_SHIFTS):
        selector = (shift_table == offset).astype(jnp.bfloat16)
        window = series[:, :, :, offset * TILE : offset * TILE + TIME]
        summed = summed + jnp.einsum(
            "gfs,bgst->gfbt", selector, window, preferred_element_type=jnp.float32
        )
    return summed.reshape(group_count * per_group, series.shape[0], TIME)


def local(intensity, chan_shift, sub_shift, widths):
    regrouped_data = lax.all_to_all(intensity, "beam", split_axis=1, concat_axis=0, tiled=True)
    beam_count = regrouped_data.shape[1]
    chan_count = regrouped_data.shape[2]
    sub_count = chan_count // CHSUB
    tiled = regrouped_data.reshape(TIME_IN, beam_count, sub_count, CHSUB)
    chan_table = chan_shift.reshape(DMG, sub_count, CHSUB)
    summed = jnp.zeros((beam_count, DMG, sub_count, MID_TILES * TILE), jnp.float32)
    for offset in range(CH_SHIFTS):
        selector = (chan_table == offset).astype(jnp.bfloat16)
        window = tiled[offset * TILE : offset * TILE + MID_TILES * TILE]
        summed = summed + jnp.einsum(
            "gsq,tbsq->bgst", selector, window, preferred_element_type=jnp.float32
        )
    subseries = summed.astype(jnp.bfloat16)
    band_index = lax.axis_index("band")
    own_rows = DMS // lax.axis_size("band")
    first_col = band_index * sub_count
    local_shifts = lax.dynamic_slice_in_dim(sub_shift, first_col, sub_count, 1)
    dm_sums = lax.psum_scatter(
        dedisperse(subseries, local_shifts), "band", scatter_dimension=0, tiled=True
    )
    dm_series = (dm_sums * (1.0 / math.sqrt(CHANNELS))).astype(jnp.bfloat16)
    values = dm_series.astype(jnp.float32)
    centre = jnp.mean(values, axis=2, keepdims=True)
    spread = jnp.mean((values - centre) ** 2, axis=2, keepdims=True)
    normed = ((values - centre) / jnp.sqrt(spread + EPSILON)).astype(jnp.bfloat16)
    normed = normed.reshape(own_rows * beam_count, TIME)
    sample_index = jnp.arange(TIME, dtype=jnp.int32)
    time_lag = sample_index[None, :] - sample_index[:, None]

    def one_width(box_width):
        kernel = ((time_lag >= 0) & (time_lag < box_width)).astype(jnp.bfloat16)
        box_sum = jnp.dot(normed, kernel, preferred_element_type=jnp.float32)
        ratio = box_sum / jnp.sqrt(box_width.astype(jnp.float32))
        return jnp.max(ratio.reshape(own_rows, beam_count, OUT_TILES, TILE), axis=(0, 3))

    local_peaks = lax.map(one_width, widths)
    snr_peak = lax.pmax(jnp.transpose(local_peaks, (1, 0, 2)), "band")
    return (dm_series, snr_peak)


def solution(mesh):
    placed = (P("beam", None, "band"), P(None, "band"), P(), P())
    return jax.shard_map(
        local,
        mesh=mesh,
        in_specs=placed,
        out_specs=(P("band", "beam", None), P("beam", None, None)),
        check_vma=False,
    )
```

profile of v0, /device:TPU:1, one launch (start us, length us, event | category | flops | bytes accessed | tf_op | source)
XLA Modules:
  0.0 223.8 jit_solution(2971477771031765155)
XLA Ops:
  7.2 2.4 %copy.86 = bf16[40,32,256]{2,0,1:T(8,128)(2,1)} copy(bf16[40,32,256]{2,1,0:T(8,128)(2,1)} %param.6) | data formatting | bytes 1310720 | tf_op args[0]
  9.6 18.5 %all-to-all-start = ((bf16[40,32,256]{2,0,1:T(8,128)(2,1)}), bf16[40,32,256]{2,0,1:T(8,128)(2,1)S(1)}, u32[]{:S(2)}, u32[]{:S(2)}) async-start(bf16[40,32,256]{2,0,1:T(8,128)(2,1)} %copy.86), calls=%async_computation | async-start | bytes 1310720 | tf_op jit(solution)/shard_map/all_to_all | solution.py:39
  30.4 34.3 %all-to-all-done = bf16[40,32,256]{2,0,1:T(8,128)(2,1)S(1)} async-done(((bf16[40,32,256]{2,0,1:T(8,128)(2,1)}), bf16[40,32,256]{2,0,1:T(8,128)(2,1)S(1)}, u32[]{:S(2)}, u32[]{:S(2)}) %all-to-all-start) | async-done | bytes 655392 | tf_op jit(solution)/shard_map/all_to_all | solution.py:39
  64.8 0.8 copy-done.2
  65.6 3.9 %copy.87 = bf16[32,40,1,256]{1,0,3,2:T(8,128)(2,1)S(1)} copy(bf16[32,40,1,256]{3,1,0,2:T(8,128)(2,1)} %bitcast.66) | data formatting | bytes 1310720 | tf_op jit(solution)/shard_map/all_to_all | solution.py:39
  69.5 4.5 %reshape.98 = bf16[1280,1,16,16]{0,3,2,1:T(8,128)(2,1)} reshape(bf16[32,40,1,256]{1,0,3,2:T(8,128)(2,1)S(1)} %copy.87) | data formatting | bytes 1310720 | tf_op jit(solution)/shard_map/reshape | solution.py:43
  74.0 1.7 fusion.12
  79.4 2.4 %add_add_fusion = f32[32,32,512]{2,1,0:T(8,128)} fusion(f32[32,32,512]{2,1,0:T(8,128)S(1)} %fusion.14, f32[32,32,512]{2,1,0:T(8,128)S(1)} %fusion.16, f32[32,32,512]{2,1,0:T(8,128)S(1)} %fusion.18, f32[32,32,512]{2,1,0:T(8,128)S(1)} %fusion.22, f32[32,32,512]{2,1,0:T(8,128)S(1)} %fusion.20, bf16[32,16,512]{2,0,1:T(8,128)(2,1)S(1)} %get-tuple-element.67, ...), kind=kOutput, calls=%fused_computation.15 | convolution fusion | flops 19398656 | bytes 13123584 | tf_op jit(solution)/shard_map/gfs,bgst->gfbt/dot_general | solution.py:32
  81.8 62.2 %reduce-scatter.2.cloned.1.call-done = f32[64,1,512]{2,0,1:T(8,128)} async-done(((f32[1024,1,512]{2,0,1:T(8,128)}), f32[64,1,512]{2,0,1:T(8,128)}) %reduce-scatter.2.cloned.1.call-update) | async-done | bytes 131088 | tf_op jit(solution)/shard_map/reduce_scatter | solution.py:57
  144.0 1.0 convert_reduce_fusion
  145.7 40.9 %while.12 = (s32[]{:T(128)}, f32[16,1,4]{2,1,0:T(1,128)S(1)}, s32[16]{0:T(128)S(1)}, bf16[64,512]{1,0:T(8,128)(2,1)S(1)}, s32[]{:T(128)}) while((s32[]{:T(128)}, f32[16,1,4]{2,1,0:T(1,128)S(1)}, s32[16]{0:T(128)S(1)}, bf16[64,512]{1,0:T(8,128)(2,1)S(1)}, s32[]{:T(128)}) %tuple.45), condition=%wide.region_6.7_spmd.clone.clone, body=%wide.region_3.6_spmd.clone.clone.sunk | while | flops 34668540 | bytes 70773 | solution.py:75
  147.1 1.0 fusion.43
  148.2 0.7 dynamic_slice.12
  149.7 1.0 fusion.43
  150.8 0.7 dynamic_slice.12
  152.2 1.0 fusion.43
  153.4 0.7 dynamic_slice.12
  154.8 1.0 fusion.43
  155.9 0.7 dynamic_slice.12
  157.3 1.0 fusion.43
  159.9 1.0 fusion.43
  162.4 1.0 fusion.43
  165.0 1.0 fusion.43
  167.5 1.0 fusion.43
  170.1 1.0 fusion.43
  172.6 1.0 fusion.43
  175.2 1.0 fusion.43
  177.8 1.0 fusion.43
  180.3 1.0 fusion.43
  182.9 1.0 fusion.43
  185.4 1.0 fusion.43
  186.6 30.3 %pmax.7 = f32[1,16,4]{1,2,0:T(4,128)} all-reduce(f32[1,16,4]{1,2,0:T(4,128)S(1)} %bitcast.69), channel_id=1, replica_groups=mesh['beam'=32,'band'=16] {'band'}, use_global_device_ids=true, to_apply=%region_7.8 | all-reduce | flops 64 | bytes 512 | tf_op jit(solution)/shard_map/pmax | solution.py:76
  (83 shorter events, 16.7 us)
Async XLA Ops:
  7.2 20.9 %copy-start = (s32[1024,256]{1,0:T(8,128)S(1)}, s32[1024,256]{1,0:T(8,128)}, u32[]{:S(2)}) copy-start(s32[1024,256]{1,0:T(8,128)} %param.8) | copy-start | bytes 3145732
  7.2 21.6 %copy-start.5 = (s32[32,256]{1,0:T(8,128)S(1)}, s32[32,256]{1,0:T(8,128)}, u32[]{:S(2)}) copy-start(s32[32,256]{1,0:T(8,128)} %param.7) | copy-start | bytes 98308
  9.6 55.2 %all-to-all-start = ((bf16[40,32,256]{2,0,1:T(8,128)(2,1)}), bf16[40,32,256]{2,0,1:T(8,128)(2,1)S(1)}, u32[]{:S(2)}, u32[]{:S(2)}) async-start(bf16[40,32,256]{2,0,1:T(8,128)(2,1)} %copy.86), calls=%async_computation | async-start | bytes 1310720 | tf_op jit(solution)/shard_map/all_to_all | solution.py:39
  28.1 116.0 %reduce-scatter.2.cloned.1.call-start = ((), (), s32[]{:S(2)}) async-start(), calls=%async_computation.2 | async-start | bytes 2228224 | tf_op jit(solution)/shard_map/reduce_scatter | solution.py:57
  64.8 0.8 copy-start.2
  74.0 1.7 copy-start.1
  74.0 1.7 copy-start.4
  81.8 63.6 %copy-start.6 = (s32[16]{0:T(128)S(1)}, s32[16]{0:T(128)}, u32[]{:S(2)}) copy-start(s32[16]{0:T(128)} %param.9) | copy-start | bytes 196
  145.1 0.6 copy-start.3
Sparse Core Ops, SparseCore 0:
  81.9 62.0 reduce-scatter.1
where the time goes:
time: 224 us
  waiting for transfers between devices  96.6 us (43%)
  blocking collectives  30.3 us (14%)
  local copies, waits for them, and re-layouts  24.7 us (11%)
  matrix products  23.4 us (10%)
  starting transfers between devices  18.5 us (8%)
  between operations  14.3 us (6%)
  loops' own time  12.1 us (5%)
  other arithmetic  3.87 us (2%)
    reduce_scatter x1, waiting for transfers between devices, local(): lax.psum_scatter(dedisperse(subseries, local_shifts), 'band', scatter_dim...  62.2 us
    all_to_all x1, waiting for transfers between devices, local(): lax.all_to_all(intensity, 'beam', split_axis=1, concat_axis=0, tiled=True)  34.3 us
    pmax x1, blocking collectives, local(): snr_peak = lax.pmax(jnp.transpose(local_peaks, (1, 0, 2)), 'band')  30.3 us
    all_to_all x1, starting transfers between devices, local(): lax.all_to_all(intensity, 'beam', split_axis=1, concat_axis=0, tiled=True)  18.5 us
    dot_general x16, matrix products, one_width(): box_sum = jnp.dot(normed, kernel, preferred_element_type=jnp.float32)  16.1 us
    another operation x1, loops' own time, local(): local_peaks = lax.map(one_width, widths)  12.1 us
    dynamic_slice x16, local copies, waits for them, and re-layouts, local(): local_peaks = lax.map(one_width, widths)  10.7 us
    dot_general x6, matrix products, dedisperse(): jnp.einsum('gfs,bgst->gfbt', selector, window, preferred_element_type=jnp...  5.13 us
  transfers between devices with their start and end apart: 2, of which 2 were waited for; matrix products, arithmetic and copies ran while one was open for 1% of the time, Pallas kernels for 0%

commit v1 on v0

v1 whole, which is shorter than its diff:
```python
import jax
import jax.numpy as jnp
from jax import lax
from jax.experimental import pallas as pl
from jax.experimental.pallas import tpu as pltpu
from jax.sharding import PartitionSpec as P

MESH = pl.DeviceIdType.MESH
F32 = jnp.float32
BF16 = jnp.bfloat16
LANES = 128
SAMPLES = 40
BEAMS = 32
BANDS = 16
HALVES = 2
GROUPS = 32
SUB_ROWS = 16
TILES_IN = 10
TILES_MID = 9
TILES_OUT = 4
SHIFTS = 6
OWN = 64
NBOX = 16
EPSILON = 1e-05


def dot(a, b):
    return lax.dot_general(a, b, (((1,), (0,)), ((), ())), preferred_element_type=F32)


def dot_t(a, b):
    return lax.dot_general(a, b, (((1,), (1,)), ((), ())), preferred_element_type=F32)


def kernel(
    x_ref, chan_ref, shift_ref, width_ref, dm_ref, peak_ref,
    wide, block, got, chan_sel, shift_own, shift_sel, series, held, box, root, total, peaks, peaks_in,
    load_sem, beam_send, beam_recv, band_send, band_recv, peak_send, peak_recv,
):
    me = lax.axis_index("beam")
    band = lax.axis_index("band")

    barrier = pltpu.get_barrier_semaphore()

    def greet_beam(i, _):
        pl.semaphore_signal(barrier, inc=1, device_id=(lax.rem(me + i, BEAMS), band), device_id_type=MESH)
        return 0

    def greet_band(i, _):
        pl.semaphore_signal(barrier, inc=1, device_id=(me, lax.rem(band + i, BANDS)), device_id_type=MESH)
        return 0

    lax.fori_loop(1, BEAMS, greet_beam, 0)
    lax.fori_loop(1, BANDS, greet_band, 0)

    own_shift = pltpu.make_async_copy(shift_ref.at[pl.ds(band * OWN, OWN)], shift_own, load_sem)
    own_shift.start()

    def widen(i, _):
        for h in range(HALVES):
            part = x_ref[pl.ds(i * 8, 8), :, h * LANES : (h + 1) * LANES]
            wide[h, pl.ds(pl.multiple_of(i * 8 * BEAMS, 8 * BEAMS), 8 * BEAMS), :] = part.astype(F32).reshape(8 * BEAMS, LANES)
        return 0

    lax.fori_loop(0, SAMPLES // 8, widen, 0)

    def pick(b, _):
        for h in range(HALVES):
            block[h, b] = wide.at[h][pl.ds(b, SAMPLES, stride=BEAMS), :].astype(BF16)
        return 0

    lax.fori_loop(0, BEAMS, pick, 0)

    pl.semaphore_wait(barrier, BEAMS - 1 + BANDS - 1)

    for h in range(HALVES):
        def send_beam(i, _):
            peer = lax.rem(me + i, BEAMS)
            pltpu.make_async_remote_copy(
                src_ref=block.at[h, peer], dst_ref=got.at[h, me],
                send_sem=beam_send.at[h], recv_sem=beam_recv.at[h],
                device_id=(peer, band), device_id_type=MESH,
            ).start()
            return 0

        lax.fori_loop(1, BEAMS, send_beam, 0)
        got[h, me] = block[h, me]

    row = lax.broadcasted_iota(jnp.int32, (GROUPS * 8, LANES), 0)
    lane = lax.broadcasted_iota(jnp.int32, (GROUPS * 8, LANES), 1)
    mine = lax.rem(row, 8) == lane // 16
    for h in range(HALVES):
        delays = chan_ref[:, h * LANES : (h + 1) * LANES]
        delays = jnp.broadcast_to(delays[:, None, :], (GROUPS, 8, LANES)).reshape(GROUPS * 8, LANES)
        for k in range(2):
            chan_sel[h, :, k * LANES : (k + 1) * LANES] = jnp.where(mine & (delays == k), 1.0, 0.0).astype(BF16)

    own_shift.wait()
    col = lax.broadcasted_iota(jnp.int32, (32, 256), 1)
    high = lax.rem(col // 8, 2) == 1
    for h in range(HALVES):
        first, second = shift_own[0:32, :], shift_own[32:64, :]
        if h == 0:
            second = pltpu.roll(second, 8, 1)
        else:
            first = pltpu.roll(first, 256 - 8, 1)
        for k in range(SHIFTS):
            shift_sel[h, k * OWN : k * OWN + 32, :] = jnp.where((first == k) & jnp.logical_not(high), 1.0, 0.0).astype(BF16)
            shift_sel[h, k * OWN + 32 : (k + 1) * OWN, :] = jnp.where((second == k) & high, 1.0, 0.0).astype(BF16)

    lag = (
        lax.broadcasted_iota(jnp.int32, (256, LANES), 1) + LANES
        - lax.broadcasted_iota(jnp.int32, (256, LANES), 0)
    )
    which = lax.broadcasted_iota(jnp.int32, (NBOX, LANES), 0)
    scale = jnp.ones((NBOX, LANES), F32)
    for i in range(NBOX):
        width = width_ref[i]
        box[:, i * LANES : (i + 1) * LANES] = jnp.where((lag >= 0) & (lag < width), 1.0, 0.0).astype(BF16)
        scale = jnp.where(which == i, width.astype(F32), scale)
    root[...] = jnp.sqrt(scale)

    total[...] = jnp.zeros_like(total)

    def arrived(buffer, sem):
        pltpu.make_async_copy(buffer, buffer, sem).wait()

    def subseries(h):
        arrived(got.at[h, pl.ds(0, BEAMS - 1)], beam_recv.at[h])
        data = got[h].astype(F32).reshape(BEAMS * SAMPLES, LANES).astype(BF16)
        for first, count in ((0, 4), (4, 5)):
            rows = count * LANES
            pair = jnp.concatenate(
                [data[first * LANES : first * LANES + rows], data[(first + 1) * LANES : (first + 1) * LANES + rows]], axis=1
            )
            summed = dot_t(chan_sel[h], pair).astype(BF16)
            for i in range(count):
                series[h, :, first + i] = summed[:, i * LANES : (i + 1) * LANES].reshape(BANDS, SUB_ROWS, LANES)

        def send_band(i, _):
            peer = lax.rem(band + i, BANDS)
            pltpu.make_async_remote_copy(
                src_ref=series.at[h, peer], dst_ref=held.at[h, band],
                send_sem=band_send.at[h], recv_sem=band_recv.at[h],
                device_id=(me, peer), device_id_type=MESH,
            ).start()
            return 0

        lax.fori_loop(1, BANDS, send_band, 0)
        held[h, band] = series[h, band]

    def trials(h):
        arrived(held.at[h, pl.ds(0, BANDS - 1)], band_recv.at[h])
        for tile in range(0, TILES_MID, 2):
            tiles = [t for t in (tile, tile + 1) if t < TILES_MID]
            low = max(0, tiles[0] - TILES_OUT + 1)
            top = min(SHIFTS - 1, tiles[-1])
            data = jnp.concatenate([held[h, :, t].reshape(BANDS * SUB_ROWS, LANES) for t in tiles], axis=1)
            part = dot(shift_sel[h, low * OWN : (top + 1) * OWN, :], data)
            for n, t in enumerate(tiles):
                for k in range(low, top + 1):
                    o = t - k
                    if 0 <= o < TILES_OUT:
                        total[:, o * LANES : (o + 1) * LANES] += part[
                            (k - low) * OWN : (k - low + 1) * OWN, n * LANES : (n + 1) * LANES
                        ]

    subseries(0)
    trials(0)
    subseries(1)
    trials(1)

    dm = (total[...] * (1.0 / 64.0)).astype(BF16)
    dm_ref[...] = dm
    values = dm.astype(F32)
    centre = jnp.mean(values, axis=1, keepdims=True)
    off = values - centre
    spread = jnp.mean(off * off, axis=1, keepdims=True)
    normed = (off / jnp.sqrt(spread + EPSILON)).astype(BF16)
    before = jnp.concatenate([jnp.zeros((OWN, LANES), BF16), normed[:, : 3 * LANES]], axis=1)
    pairs = jnp.concatenate(
        [
            jnp.concatenate([before[:, k * LANES : (k + 1) * LANES], normed[:, k * LANES : (k + 1) * LANES]], axis=1)
            for k in range(TILES_OUT)
        ],
        axis=0,
    )
    best = [[] for _ in range(TILES_OUT)]
    for i in range(0, NBOX, 2):
        sums = dot(pairs, box[:, i * LANES : (i + 2) * LANES])
        for k in range(TILES_OUT):
            top = jnp.max(sums[k * OWN : (k + 1) * OWN].reshape(8, 8, 2 * LANES), axis=0)
            best[k] += [top[:, :LANES], top[:, LANES:]]
    place = lax.broadcasted_iota(jnp.int32, (NBOX, LANES), 1)
    found = jnp.zeros((NBOX, LANES), F32)
    for k in range(TILES_OUT):
        rows = jnp.max(jnp.stack(best[k], axis=0), axis=1)
        found = jnp.where(place == k, jnp.max(rows, axis=1, keepdims=True), found)
    peaks[...] = found / root[...]

    def send_peak(i, _):
        peer = lax.rem(band + i, BANDS)
        pltpu.make_async_remote_copy(
            src_ref=peaks, dst_ref=peaks_in.at[band],
            send_sem=peak_send, recv_sem=peak_recv,
            device_id=(me, peer), device_id_type=MESH,
        ).start()
        return 0

    lax.fori_loop(1, BANDS, send_peak, 0)
    peaks_in[band] = peaks[...]
    for h in range(HALVES):
        arrived(block.at[h, pl.ds(0, BEAMS - 1)], beam_send.at[h])
        arrived(series.at[h, pl.ds(0, BANDS - 1)], band_send.at[h])
    arrived(peaks_in.at[pl.ds(0, BANDS - 1)], peak_recv)
    peak_ref[...] = jnp.max(peaks_in[...], axis=0)[:, :TILES_OUT]
    arrived(peaks_in.at[pl.ds(0, BANDS - 1)], peak_send)


def local(intensity, chan_shift, sub_shift, widths):
    vmem = pl.BlockSpec(memory_space=pltpu.VMEM)
    dm, peak = pl.pallas_call(
        kernel,
        out_shape=(
            jax.ShapeDtypeStruct((OWN, TILES_OUT * LANES), BF16),
            jax.ShapeDtypeStruct((NBOX, TILES_OUT), F32),
        ),
        in_specs=[vmem, vmem, pl.BlockSpec(memory_space=pl.ANY), pl.BlockSpec(memory_space=pltpu.SMEM)],
        out_specs=(vmem, vmem),
        scratch_shapes=[
            pltpu.VMEM((HALVES, SAMPLES * BEAMS, LANES), F32),
            pltpu.VMEM((HALVES, BEAMS, SAMPLES, LANES), BF16),
            pltpu.VMEM((HALVES, BEAMS, SAMPLES, LANES), BF16),
            pltpu.VMEM((HALVES, GROUPS * 8, 2 * LANES), BF16),
            pltpu.VMEM((OWN, 256), jnp.int32),
            pltpu.VMEM((HALVES, SHIFTS * OWN, 256), BF16),
            pltpu.VMEM((HALVES, BANDS, TILES_MID, SUB_ROWS, LANES), BF16),
            pltpu.VMEM((HALVES, BANDS, TILES_MID, SUB_ROWS, LANES), BF16),
            pltpu.VMEM((256, NBOX * LANES), BF16),
            pltpu.VMEM((NBOX, LANES), F32),
            pltpu.VMEM((OWN, TILES_OUT * LANES), F32),
            pltpu.VMEM((NBOX, LANES), F32),
            pltpu.VMEM((BANDS, NBOX, LANES), F32),
            pltpu.SemaphoreType.DMA,
            pltpu.SemaphoreType.DMA((HALVES,)),
            pltpu.SemaphoreType.DMA((HALVES,)),
            pltpu.SemaphoreType.DMA((HALVES,)),
            pltpu.SemaphoreType.DMA((HALVES,)),
            pltpu.SemaphoreType.DMA,
            pltpu.SemaphoreType.DMA,
        ],
        compiler_params=pltpu.CompilerParams(
            collective_id=0, has_side_effects=True, vmem_limit_bytes=48 << 20
        ),
        cost_estimate=pl.CostEstimate(flops=4_000_000_000, bytes_accessed=2_000_000, transcendentals=0),
    )(intensity, chan_shift, sub_shift, widths)
    return dm.reshape(OWN, 1, TILES_OUT * LANES), peak.reshape(1, NBOX, TILES_OUT)


def solution(mesh):
    return jax.shard_map(
        local,
        mesh=mesh,
        in_specs=(P("beam", None, "band"), P(None, "band"), P(), P()),
        out_specs=(P("band", "beam", None), P("beam", None, None)),
        check_vma=False,
    )
```

time: 224 us -> 67.4 us (0.30)
  waiting for transfers between devices: 96.6 us -> 0 us
  Pallas kernels: 0 us -> 61.5 us
  blocking collectives: 30.3 us -> 0 us
  matrix products: 23.4 us -> 0 us
  local copies, waits for them, and re-layouts: 24.7 us -> 5 us
  starting transfers between devices: 18.5 us -> 0 us
  between operations: 14.3 us -> 0.65 us
  loops' own time: 12.1 us -> 0 us
  other arithmetic: 3.87 us -> 0 us
    reduce_scatter x1 -> x0, waiting for transfers between devices: 62.2 us -> none  [local(): lax.psum_scatter(dedisperse(subseries, local_shifts), 'band', scatter_dim...]
    pallas_call x0 -> x1, Pallas kernels: none -> 61.5 us  [local(): pl.pallas_call(kernel, out_shape=(jax.ShapeDtypeStruct((OWN, TILES_OUT *...]
    all_to_all x1 -> x0, waiting for transfers between devices: 34.3 us -> none  [local(): lax.all_to_all(intensity, 'beam', split_axis=1, concat_axis=0, tiled=True)]
    pmax x1 -> x0, blocking collectives: 30.3 us -> none  [local(): snr_peak = lax.pmax(jnp.transpose(local_peaks, (1, 0, 2)), 'band')]
    dot_general x24 -> x0, matrix products: 23.4 us -> none  [the longest x16 16.1 us: one_width(): box_sum = jnp.dot(normed, kernel, preferred_element_type=jnp.float32)]
    all_to_all x1 -> x0, starting transfers between devices: 18.5 us -> none  [local(): lax.all_to_all(intensity, 'beam', split_axis=1, concat_axis=0, tiled=True)]
    another operation x1 -> x0, loops' own time: 12.1 us -> none  [local(): local_peaks = lax.map(one_width, widths)]
    dynamic_slice x17 -> x0, local copies, waits for them, and re-layouts: 10.9 us -> none  [the longest x16 10.7 us: local(): local_peaks = lax.map(one_width, widths)]
  transfers between devices with their start and end apart: 2 -> 0, of which waited for: 2 -> 0; matrix products, arithmetic and copies ran while one was open for 1% -> 0% of each run, Pallas kernels for 0% -> 0%
where the time goes in v1:
time: 67.4 us; the launch traced here: 67.1 us
  Pallas kernels  61.5 us (91%)
  local copies, waits for them, and re-layouts  5 us (7%)
    pallas_call x1, Pallas kernels, local(): pl.pallas_call(kernel, out_shape=(jax.ShapeDtypeStruct((OWN, TILES_OUT *...  61.5 us
    unnamed x9, local copies, waits for them, and re-layouts  4.35 us

profile of v1, /device:TPU:1, one launch (start us, length us, event | category | flops | bytes accessed | tf_op | source)
XLA Modules:
  0.0 67.1 jit_solution(8314838946928184297)
XLA Ops:
  0.6 0.0 copy-start
  0.6 1.2 %copy-done = s32[1024,256]{1,0:T(8,128)S(1)} copy-done((s32[1024,256]{1,0:T(8,128)S(1)}, s32[1024,256]{1,0:T(8,128)}, u32[]{:S(2)}) %copy-start) | copy-done | bytes 1048600
  1.9 0.0 copy-start.1
  1.9 1.1 %copy-done.1 = bf16[40,32,256]{2,1,0:T(8,128)(2,1)S(1)} copy-done((bf16[40,32,256]{2,1,0:T(8,128)(2,1)S(1)}, bf16[40,32,256]{2,1,0:T(8,128)(2,1)}, u32[]{:S(2)}) %copy-start.1) | copy-done | bytes 655384
  2.9 0.0 copy-start.2
  2.9 0.8 %copy-done.2 = s32[32,256]{1,0:T(8,128)S(1)} copy-done((s32[32,256]{1,0:T(8,128)S(1)}, s32[32,256]{1,0:T(8,128)}, u32[]{:S(2)}) %copy-start.2) | copy-done | bytes 32792
  3.7 0.0 copy-start.3
  3.7 0.7 copy-done.3
  4.4 61.5 %shard_map.59 = (bf16[64,512]{1,0:T(8,128)(2,1)S(1)}, f32[16,4]{1,0:T(8,128)S(1)}) custom-call(bf16[40,32,256]{2,1,0:T(8,128)(2,1)S(1)} %copy-done.1, s32[32,256]{1,0:T(8,128)S(1)} %copy-done.2, s32[1024,256]{1,0:T(8,128)S(1)} %copy-done, s32[16]{0:T(128)S(1)} %copy-done.3), custom_call_target="tpu_custom_call" | custom-call | flops 4000000000 | bytes 2000000 | tf_op jit(solution)/shard_map/pallas_call | solution.py:222
  65.8 0.7 copy.6
  66.5 0.6 copy.8
Async XLA Ops:
  0.6 1.2 %copy-start = (s32[1024,256]{1,0:T(8,128)S(1)}, s32[1024,256]{1,0:T(8,128)}, u32[]{:S(2)}) copy-start(s32[1024,256]{1,0:T(8,128)} %shift_ref.1) | copy-start | bytes 3145732
  1.9 1.1 %copy-start.1 = (bf16[40,32,256]{2,1,0:T(8,128)(2,1)S(1)}, bf16[40,32,256]{2,1,0:T(8,128)(2,1)}, u32[]{:S(2)}) copy-start(bf16[40,32,256]{2,1,0:T(8,128)(2,1)} %x_ref.1) | copy-start | bytes 1966084
  2.9 0.8 %copy-start.2 = (s32[32,256]{1,0:T(8,128)S(1)}, s32[32,256]{1,0:T(8,128)}, u32[]{:S(2)}) copy-start(s32[32,256]{1,0:T(8,128)} %chan_ref.1) | copy-start | bytes 98308
  3.7 0.7 copy-start.3

commit v2 on v1

v2 whole, which is shorter than its diff:
```python
import jax
import jax.numpy as jnp
from jax import lax
from jax.experimental import pallas as pl
from jax.experimental.pallas import tpu as pltpu
from jax.sharding import PartitionSpec as P

MESH = pl.DeviceIdType.MESH
F32 = jnp.float32
BF16 = jnp.bfloat16
LANES = 128
SAMPLES = 40
BEAMS = 32
RING = 16
BANDS = 16
HALVES = 2
GROUPS = 32
SUB_ROWS = 16
TILES_IN = 10
TILES_MID = 9
TILES_OUT = 4
SHIFTS = 6
OWN = 64
NBOX = 16
EPSILON = 1e-05


def dot(a, b):
    return lax.dot_general(a, b, (((1,), (0,)), ((), ())), preferred_element_type=F32)


def dot_t(a, b):
    return lax.dot_general(a, b, (((1,), (1,)), ((), ())), preferred_element_type=F32)


def kernel(
    x_hbm, chan_hbm, shift_hbm, width_hbm, dm_ref, peak_ref,
    x_ref, chan_ref, width_ref, wide, block, got, chan_sel, shift_own, shift_sel, series, held, box, root, total, peaks, peaks_in,
    load_sem, beam_send, beam_recv, band_send, band_recv, peak_send, peak_recv,
):
    me = lax.axis_index("beam")
    band = lax.axis_index("band")
    column = me // RING
    place = lax.rem(me, RING)

    band_x, band_y, core = band // 8, lax.rem(band // 2, 4), lax.rem(band, 2)
    band_peers = [
        lax.rem(band_x + x, 2) * 8 + lax.rem(band_y + y, 4) * 2 + lax.rem(core + c, 2)
        for x, y in ((1, 2), (1, 1), (1, 3), (0, 2), (1, 0), (0, 1), (0, 3), (0, 0))
        for c in (0, 1)
        if x or y or c
    ]

    barrier = pltpu.get_barrier_semaphore()

    def greet_beam(i, _):
        step = i // 2
        there = jnp.where(lax.rem(step, 2) == 1, (step + 1) // 2, lax.rem(RING - step // 2, RING))
        peer = lax.rem(column + lax.rem(i, 2), 2) * RING + there

        @pl.when(peer != me)
        def _():
            pl.semaphore_signal(barrier, inc=1, device_id=(peer, band), device_id_type=MESH)

        return 0

    lax.fori_loop(0, BEAMS, greet_beam, 0)

    def greet_band(i, _):
        pl.semaphore_signal(barrier, inc=1, device_id=(me, lax.rem(band + i, BANDS)), device_id_type=MESH)
        return 0

    lax.fori_loop(1, BANDS, greet_band, 0)

    loads = [
        pltpu.make_async_copy(x_hbm.at[:, :, pl.ds(h * LANES, LANES)], x_ref.at[h], load_sem.at[h]) for h in range(HALVES)
    ] + [
        pltpu.make_async_copy(chan_hbm, chan_ref, load_sem.at[2]),
        pltpu.make_async_copy(shift_hbm.at[pl.ds(band * OWN, OWN)], shift_own, load_sem.at[3]),
        pltpu.make_async_copy(width_hbm, width_ref, load_sem.at[4]),
    ]
    for load in loads:
        load.start()

    def gather(h):
        loads[h].wait()

        def widen(i, _):
            rows = pl.ds(pl.multiple_of(i * 8 * BEAMS, 8 * BEAMS), 8 * BEAMS)
            wide[h, rows, :] = x_ref[h, pl.ds(i * 8, 8)].astype(F32).reshape(8 * BEAMS, LANES)
            return 0

        lax.fori_loop(0, SAMPLES // 8, widen, 0)

        def pick(b, _):
            block[h, b] = wide.at[h][pl.ds(b, SAMPLES, stride=BEAMS), :].astype(BF16)
            return 0

        lax.fori_loop(0, BEAMS, pick, 0, unroll=4)
        got[h, me] = block[h, me]

    gather(0)
    pl.semaphore_wait(barrier, BEAMS - 1 + BANDS - 1)

    def send_beams(h, other):
        def send(i, _):
            peer = lax.rem(column + other, 2) * RING + lax.rem(place + i, RING)
            pltpu.make_async_remote_copy(
                src_ref=block.at[h, peer], dst_ref=got.at[h, me],
                send_sem=beam_send.at[h], recv_sem=beam_recv.at[h, other],
                device_id=(peer, band), device_id_type=MESH,
            ).start()
            return 0

        lax.fori_loop(1 - other, RING, send, 0)

    send_beams(0, 0)
    send_beams(0, 1)
    gather(1)
    send_beams(1, 0)
    send_beams(1, 1)

    loads[2].wait()
    loads[3].wait()
    loads[4].wait()

    row = lax.broadcasted_iota(jnp.int32, (GROUPS * 8, LANES), 0)
    lane = lax.broadcasted_iota(jnp.int32, (GROUPS * 8, LANES), 1)
    mine = lax.rem(row, 8) == lane // 16
    for h in range(HALVES):
        delays = chan_ref[:, h * LANES : (h + 1) * LANES]
        delays = jnp.broadcast_to(delays[:, None, :], (GROUPS, 8, LANES)).reshape(GROUPS * 8, LANES)
        for k in range(2):
            chan_sel[h, :, k * LANES : (k + 1) * LANES] = jnp.where(mine & (delays == k), 1.0, 0.0).astype(BF16)

    col = lax.broadcasted_iota(jnp.int32, (32, 256), 1)
    high = lax.rem(col // 8, 2) == 1
    for h in range(HALVES):
        first, second = shift_own[0:32, :], shift_own[32:64, :]
        if h == 0:
            second = pltpu.roll(second, 8, 1)
        else:
            first = pltpu.roll(first, 256 - 8, 1)
        for k in range(SHIFTS):
            shift_sel[h, k * OWN : k * OWN + 32, :] = jnp.where((first == k) & jnp.logical_not(high), 1.0, 0.0).astype(BF16)
            shift_sel[h, k * OWN + 32 : (k + 1) * OWN, :] = jnp.where((second == k) & high, 1.0, 0.0).astype(BF16)

    lag = (
        lax.broadcasted_iota(jnp.int32, (256, LANES), 1) + LANES
        - lax.broadcasted_iota(jnp.int32, (256, LANES), 0)
    )
    which = lax.broadcasted_iota(jnp.int32, (8, LANES), 1)
    scale = jnp.ones((8, LANES), F32)
    for i in range(NBOX):
        width = width_ref[i]
        box[:, i * LANES : (i + 1) * LANES] = jnp.where((lag >= 0) & (lag < width), 1.0, 0.0).astype(BF16)
        scale = jnp.where(which == i, width.astype(F32), scale)
    root[...] = jnp.sqrt(scale)

    total[...] = jnp.zeros_like(total)

    def arrived(buffer, sem):
        pltpu.make_async_copy(buffer, buffer, sem).wait()

    def tiles_of(h, side):
        return got[h, side * RING : (side + 1) * RING].astype(F32).reshape(RING * SAMPLES, LANES).astype(BF16)

    def channel_sum(h, now, later):
        return dot_t(chan_sel[h], jnp.concatenate([now, later], axis=1)).astype(BF16)

    def keep(h, first, summed):
        for i in range(summed.shape[1] // LANES):
            series[h, :, first + i] = summed[:, i * LANES : (i + 1) * LANES].reshape(BANDS, SUB_ROWS, LANES)

    def inner_tiles(h, side):
        data = got[h, pl.ds(side * RING, RING)].astype(F32).reshape(RING * SAMPLES, LANES).astype(BF16)
        keep(h, 5 * side, channel_sum(h, data[: 4 * LANES], data[LANES:]))

    def send_series(h, part, first, count):
        for peer in band_peers:
            pltpu.make_async_remote_copy(
                src_ref=series.at[h, peer, pl.ds(first, count)], dst_ref=held.at[h, band, pl.ds(first, count)],
                send_sem=band_send.at[h], recv_sem=band_recv.at[h, part],
                device_id=(me, peer), device_id_type=MESH,
            ).start()
        held[h, band, pl.ds(first, count)] = series[h, band, pl.ds(first, count)]

    def subseries(h):
        arrived(got.at[h, pl.ds(0, RING - 1)], beam_recv.at[h, 0])
        inner_tiles(h, column)
        send_series(h, 0, 5 * column, 4)
        arrived(got.at[h, pl.ds(0, RING)], beam_recv.at[h, 1])
        inner_tiles(h, 1 - column)
        keep(h, 4, channel_sum(h, tiles_of(h, 0)[4 * LANES :], tiles_of(h, 1)[:LANES]))
        send_series(h, 1, 4 * (1 - column), 5)

    def trials(h):
        arrived(held.at[h, pl.ds(0, BANDS - 1), pl.ds(0, 4)], band_recv.at[h, 0])
        arrived(held.at[h, pl.ds(0, BANDS - 1), pl.ds(0, 5)], band_recv.at[h, 1])
        for tile in range(0, TILES_MID, 2):
            tiles = [t for t in (tile, tile + 1) if t < TILES_MID]
            low = max(0, tiles[0] - TILES_OUT + 1)
            top = min(SHIFTS - 1, tiles[-1])
            data = jnp.concatenate([held[h, :, t].reshape(BANDS * SUB_ROWS, LANES) for t in tiles], axis=1)
            part = dot(shift_sel[h, low * OWN : (top + 1) * OWN, :], data)
            for n, t in enumerate(tiles):
                for k in range(low, top + 1):
                    o = t - k
                    if 0 <= o < TILES_OUT:
                        total[:, o * LANES : (o + 1) * LANES] += part[
                            (k - low) * OWN : (k - low + 1) * OWN, n * LANES : (n + 1) * LANES
                        ]

    subseries(0)
    trials(0)
    subseries(1)
    trials(1)

    dm = (total[...] * (1.0 / 64.0)).astype(BF16)
    dm_ref[...] = dm
    values = dm.astype(F32)
    centre = jnp.mean(values, axis=1, keepdims=True)
    off = values - centre
    spread = jnp.mean(off * off, axis=1, keepdims=True)
    normed = (off / jnp.sqrt(spread + EPSILON)).astype(BF16)
    before = jnp.concatenate([jnp.zeros((OWN, LANES), BF16), normed[:, : 3 * LANES]], axis=1)
    pairs = jnp.concatenate(
        [
            jnp.concatenate([before[:, k * LANES : (k + 1) * LANES], normed[:, k * LANES : (k + 1) * LANES]], axis=1)
            for k in range(TILES_OUT)
        ],
        axis=0,
    )
    best = [[] for _ in range(TILES_OUT)]
    for i in range(0, NBOX, 2):
        sums = dot(pairs, box[:, i * LANES : (i + 2) * LANES])
        for k in range(TILES_OUT):
            top = jnp.max(sums[k * OWN : (k + 1) * OWN].reshape(8, 8, 2 * LANES), axis=0)
            best[k] += [top[:, :LANES], top[:, LANES:]]
    rows = jnp.concatenate([jnp.max(jnp.stack(best[k], axis=0), axis=1) for k in range(TILES_OUT)] * 2, axis=0)
    found = jnp.max(rows.T, axis=0, keepdims=True)
    found = jnp.concatenate([found if k == 0 else pltpu.roll(found, LANES - k * NBOX, 1) for k in range(TILES_OUT)] * 2, axis=0)
    peaks[...] = found / root[...]

    for peer in band_peers:
        pltpu.make_async_remote_copy(
            src_ref=peaks, dst_ref=peaks_in.at[band],
            send_sem=peak_send, recv_sem=peak_recv,
            device_id=(me, peer), device_id_type=MESH,
        ).start()
    peaks_in[band] = peaks[...]
    for h in range(HALVES):
        arrived(block.at[h, pl.ds(0, BEAMS - 1)], beam_send.at[h])
        arrived(series.at[h, pl.ds(0, BANDS - 1)], band_send.at[h])
    arrived(peaks_in.at[pl.ds(0, BANDS - 1)], peak_recv)
    peak_ref[...] = jnp.max(peaks_in[...], axis=0)[:TILES_OUT, :NBOX]
    arrived(peaks_in.at[pl.ds(0, BANDS - 1)], peak_send)


def local(intensity, chan_shift, sub_shift, widths):
    vmem = pl.BlockSpec(memory_space=pltpu.VMEM)
    operands = [pltpu.with_memory_space_constraint(a, pltpu.HBM) for a in (intensity, chan_shift, sub_shift, widths)]
    dm, peak = pl.pallas_call(
        kernel,
        out_shape=(
            jax.ShapeDtypeStruct((OWN, TILES_OUT * LANES), BF16),
            jax.ShapeDtypeStruct((TILES_OUT, NBOX), F32),
        ),
        in_specs=[pl.BlockSpec(memory_space=pltpu.HBM)] * 4,
        out_specs=(vmem, vmem),
        scratch_shapes=[
            pltpu.VMEM((HALVES, SAMPLES, BEAMS, LANES), BF16),
            pltpu.VMEM((GROUPS, 2 * LANES), jnp.int32),
            pltpu.SMEM((NBOX,), jnp.int32),
            pltpu.VMEM((HALVES, SAMPLES * BEAMS, LANES), F32),
            pltpu.VMEM((HALVES, BEAMS, SAMPLES, LANES), BF16),
            pltpu.VMEM((HALVES, BEAMS, SAMPLES, LANES), BF16),
            pltpu.VMEM((HALVES, GROUPS * 8, 2 * LANES), BF16),
            pltpu.VMEM((OWN, 256), jnp.int32),
            pltpu.VMEM((HALVES, SHIFTS * OWN, 256), BF16),
            pltpu.VMEM((HALVES, BANDS, TILES_MID, SUB_ROWS, LANES), BF16),
            pltpu.VMEM((HALVES, BANDS, TILES_MID, SUB_ROWS, LANES), BF16),
            pltpu.VMEM((256, NBOX * LANES), BF16),
            pltpu.VMEM((8, LANES), F32),
            pltpu.VMEM((OWN, TILES_OUT * LANES), F32),
            pltpu.VMEM((8, LANES), F32),
            pltpu.VMEM((BANDS, 8, LANES), F32),
            pltpu.SemaphoreType.DMA((5,)),
            pltpu.SemaphoreType.DMA((HALVES,)),
            pltpu.SemaphoreType.DMA((HALVES, 2)),
            pltpu.SemaphoreType.DMA((HALVES,)),
            pltpu.SemaphoreType.DMA((HALVES, 2)),
            pltpu.SemaphoreType.DMA,
            pltpu.SemaphoreType.DMA,
        ],
        compiler_params=pltpu.CompilerParams(
            collective_id=0, has_side_effects=True, vmem_limit_bytes=48 << 20
        ),
        cost_estimate=pl.CostEstimate(flops=4_000_000_000, bytes_accessed=2_000_000, transcendentals=0),
    )(*operands)
    return dm.reshape(OWN, 1, TILES_OUT * LANES), peak.T.reshape(1, NBOX, TILES_OUT)


def solution(mesh):
    return jax.shard_map(
        local,
        mesh=mesh,
        in_specs=(P("beam", None, "band"), P(None, "band"), P(), P()),
        out_specs=(P("band", "beam", None), P("beam", None, None)),
        check_vma=False,
    )
```

time: 67.4 us -> 62.3 us (0.924)
  local copies, waits for them, and re-layouts: 5 us -> 1.21 us
  Pallas kernels: 61.5 us -> 60.3 us
    unnamed x9 -> x2, local copies, waits for them, and re-layouts: 4.35 us -> 1.21 us
    pallas_call x1, Pallas kernels: 61.5 us -> 60.3 us  [local(): pl.pallas_call(kernel, out_shape=(jax.ShapeDtypeStruct((OWN, TILES_OUT *...]
where the time goes in v2:
time: 62.3 us; the launch traced here: 62.2 us
  Pallas kernels  60.3 us (97%)
  local copies, waits for them, and re-layouts  1.21 us (2%)
  between operations  0.64 us (1%)
    pallas_call x1, Pallas kernels, local(): pl.pallas_call(kernel, out_shape=(jax.ShapeDtypeStruct((OWN, TILES_OUT *...  60.3 us

profile of v2, /device:TPU:1, one launch (start us, length us, event | category | flops | bytes accessed | tf_op | source)
XLA Modules:
  0.0 62.2 jit_solution(13550285271510010409)
XLA Ops:
  0.6 60.3 %shard_map.59 = (bf16[64,512]{1,0:T(8,128)(2,1)S(1)}, f32[4,16]{1,0:T(4,128)S(1)}) custom-call(bf16[40,32,256]{2,1,0:T(8,128)(2,1)} %x_hbm.1, s32[32,256]{1,0:T(8,128)} %chan_hbm.1, s32[1024,256]{1,0:T(8,128)} %shift_hbm.1, s32[16]{0:T(128)} %width_hbm.1), custom_call_target="tpu_custom_call" | custom-call | flops 4000000000 | bytes 2000000 | tf_op jit(solution)/shard_map/pallas_call | solution.py:263
  61.0 0.6 %copy.8 = bf16[64,1,512]{2,0,1:T(8,128)(2,1)} copy(bf16[64,1,512]{2,0,1:T(8,128)(2,1)S(1)} %bitcast.4) | data formatting | bytes 131072
  61.6 0.6 copy.9

commit v3 on v2

--- a/solution.py
+++ b/solution.py
@@ -102,17 +102,24 @@
     gather(0)
     pl.semaphore_wait(barrier, BEAMS - 1 + BANDS - 1)
 
-    def send_beams(h, other):
+    def send_block(h, own, step):
+        peer = lax.rem(column + 1 - own, 2) * RING + lax.rem(place + step + RING, RING)
+        pltpu.make_async_remote_copy(
+            src_ref=block.at[h, peer], dst_ref=got.at[h, me],
+            send_sem=beam_send.at[h], recv_sem=beam_recv.at[h, own],
+            device_id=(peer, band), device_id_type=MESH,
+        ).start()
+
+    def send_beams(h, own):
         def send(i, _):
-            peer = lax.rem(column + other, 2) * RING + lax.rem(place + i, RING)
-            pltpu.make_async_remote_copy(
-                src_ref=block.at[h, peer], dst_ref=got.at[h, me],
-                send_sem=beam_send.at[h], recv_sem=beam_recv.at[h, other],
-                device_id=(peer, band), device_id_type=MESH,
-            ).start()
+            skip = lax.rem(RING - place, RING)
+            step = i if h == 0 else jnp.where(i == own, skip, jnp.where(i <= skip, i - 1, i))
+            if h == 1 and own:
+                step = jnp.where(place == 0, i, step)
+            send_block(h, own, step)
             return 0
 
-        lax.fori_loop(1 - other, RING, send, 0)
+        lax.fori_loop(own, RING, send, 0)
 
     send_beams(0, 0)
     send_beams(0, 1)
@@ -185,14 +192,15 @@
             ).start()
         held[h, band, pl.ds(first, count)] = series[h, band, pl.ds(first, count)]
 
-    def subseries(h):
-        arrived(got.at[h, pl.ds(0, RING - 1)], beam_recv.at[h, 0])
-        inner_tiles(h, column)
-        send_series(h, 0, 5 * column, 4)
-        arrived(got.at[h, pl.ds(0, RING)], beam_recv.at[h, 1])
-        inner_tiles(h, 1 - column)
-        keep(h, 4, channel_sum(h, tiles_of(h, 0)[4 * LANES :], tiles_of(h, 1)[:LANES]))
-        send_series(h, 1, 4 * (1 - column), 5)
+    def subseries(h, last):
+        side = column if last else 1 - column
+        arrived(got.at[h, pl.ds(0, RING - last)], beam_recv.at[h, last])
+        inner_tiles(h, side)
+        if last:
+            keep(h, 4, channel_sum(h, tiles_of(h, 0)[4 * LANES :], tiles_of(h, 1)[:LANES]))
+            send_series(h, 1, 4 * side, 5)
+        else:
+            send_series(h, 0, 5 * side, 4)
 
     def trials(h):
         arrived(held.at[h, pl.ds(0, BANDS - 1), pl.ds(0, 4)], band_recv.at[h, 0])
@@ -211,9 +219,11 @@
                             (k - low) * OWN : (k - low + 1) * OWN, n * LANES : (n + 1) * LANES
                         ]
 
-    subseries(0)
+    subseries(0, 0)
+    subseries(0, 1)
     trials(0)
-    subseries(1)
+    subseries(1, 0)
+    subseries(1, 1)
     trials(1)
 
     dm = (total[...] * (1.0 / 64.0)).astype(BF16)

time: 62.3 us -> 60.6 us (0.973)
  Pallas kernels: 60.3 us -> 58.6 us
    pallas_call x1, Pallas kernels: 60.3 us -> 58.6 us  [local(): pl.pallas_call(kernel, out_shape=(jax.ShapeDtypeStruct((OWN, TILES_OUT *...]
where the time goes in v3:
time: 60.6 us; the launch traced here: 60.4 us
  Pallas kernels  58.6 us (97%)
  local copies, waits for them, and re-layouts  1.21 us (2%)
  between operations  0.64 us (1%)
    pallas_call x1, Pallas kernels, local(): pl.pallas_call(kernel, out_shape=(jax.ShapeDtypeStruct((OWN, TILES_OUT *...  58.6 us

profile of v3, /device:TPU:1, one launch (start us, length us, event | category | flops | bytes accessed | tf_op | source)
XLA Modules:
  0.0 60.4 jit_solution(6847863480791543948)
XLA Ops:
  0.6 58.6 %shard_map.59 = (bf16[64,512]{1,0:T(8,128)(2,1)S(1)}, f32[4,16]{1,0:T(4,128)S(1)}) custom-call(bf16[40,32,256]{2,1,0:T(8,128)(2,1)} %x_hbm.1, s32[32,256]{1,0:T(8,128)} %chan_hbm.1, s32[1024,256]{1,0:T(8,128)} %shift_hbm.1, s32[16]{0:T(128)} %width_hbm.1), custom_call_target="tpu_custom_call" | custom-call | flops 4000000000 | bytes 2000000 | tf_op jit(solution)/shard_map/pallas_call | solution.py:273
  59.2 0.6 %copy.8 = bf16[64,1,512]{2,0,1:T(8,128)(2,1)} copy(bf16[64,1,512]{2,0,1:T(8,128)(2,1)S(1)} %bitcast.4) | data formatting | bytes 131072
  59.9 0.6 copy.9

commit v4 on v3

--- a/solution.py
+++ b/solution.py
@@ -36,7 +36,7 @@
 def kernel(
     x_hbm, chan_hbm, shift_hbm, width_hbm, dm_ref, peak_ref,
     x_ref, chan_ref, width_ref, wide, block, got, chan_sel, shift_own, shift_sel, series, held, box, root, total, peaks, peaks_in,
-    load_sem, beam_send, beam_recv, band_send, band_recv, peak_send, peak_recv,
+    load_sem, ready, beam_send, beam_recv, band_send, band_recv, peak_send, peak_recv,
 ):
     me = lax.axis_index("beam")
     band = lax.axis_index("band")
@@ -54,17 +54,19 @@
     barrier = pltpu.get_barrier_semaphore()
 
     def greet_beam(i, _):
-        step = i // 2
-        there = jnp.where(lax.rem(step, 2) == 1, (step + 1) // 2, lax.rem(RING - step // 2, RING))
-        peer = lax.rem(column + lax.rem(i, 2), 2) * RING + there
-
-        @pl.when(peer != me)
+        there = jnp.where(lax.rem(i, 2) == 1, (i + 1) // 2, lax.rem(RING - i // 2, RING))
+
+        @pl.when(there != place)
         def _():
-            pl.semaphore_signal(barrier, inc=1, device_id=(peer, band), device_id_type=MESH)
+            pl.semaphore_signal(barrier, inc=1, device_id=(column * RING + there, band), device_id_type=MESH)
+
+        @pl.when(column == 0)
+        def _():
+            pl.semaphore_signal(barrier, inc=1, device_id=(RING + there, band), device_id_type=MESH)
 
         return 0
 
-    lax.fori_loop(0, BEAMS, greet_beam, 0)
+    lax.fori_loop(0, RING, greet_beam, 0)
 
     def greet_band(i, _):
         pl.semaphore_signal(barrier, inc=1, device_id=(me, lax.rem(band + i, BANDS)), device_id_type=MESH)
@@ -100,7 +102,12 @@
         got[h, me] = block[h, me]
 
     gather(0)
-    pl.semaphore_wait(barrier, BEAMS - 1 + BANDS - 1)
+    pl.semaphore_wait(barrier, jnp.where(column == 0, RING, BEAMS) - 1 + BANDS - 1)
+
+    @pl.when(column == 1)
+    def _():
+        pl.semaphore_signal(ready, inc=1, device_id=(place, band), device_id_type=MESH)
+
 
     def send_block(h, own, step):
         peer = lax.rem(column + 1 - own, 2) * RING + lax.rem(place + step + RING, RING)
@@ -121,11 +128,15 @@
 
         lax.fori_loop(own, RING, send, 0)
 
-    send_beams(0, 0)
     send_beams(0, 1)
     gather(1)
+
+    @pl.when(column == 0)
+    def _():
+        pl.semaphore_wait(ready, 1)
+
+    send_beams(0, 0)
     send_beams(1, 0)
-    send_beams(1, 1)
 
     loads[2].wait()
     loads[3].wait()
@@ -192,9 +203,9 @@
             ).start()
         held[h, band, pl.ds(first, count)] = series[h, band, pl.ds(first, count)]
 
-    def subseries(h, last):
-        side = column if last else 1 - column
-        arrived(got.at[h, pl.ds(0, RING - last)], beam_recv.at[h, last])
+    def subseries(h, own, last):
+        side = column if own else 1 - column
+        arrived(got.at[h, pl.ds(0, RING - own)], beam_recv.at[h, own])
         inner_tiles(h, side)
         if last:
             keep(h, 4, channel_sum(h, tiles_of(h, 0)[4 * LANES :], tiles_of(h, 1)[:LANES]))
@@ -219,11 +230,12 @@
                             (k - low) * OWN : (k - low + 1) * OWN, n * LANES : (n + 1) * LANES
                         ]
 
-    subseries(0, 0)
-    subseries(0, 1)
+    subseries(0, 1, False)
+    send_beams(1, 1)
+    subseries(0, 0, True)
     trials(0)
-    subseries(1, 0)
-    subseries(1, 1)
+    subseries(1, 0, False)
+    subseries(1, 1, True)
     trials(1)
 
     dm = (total[...] * (1.0 / 64.0)).astype(BF16)
@@ -265,6 +277,17 @@
     arrived(peaks_in.at[pl.ds(0, BANDS - 1)], peak_recv)
     peak_ref[...] = jnp.max(peaks_in[...], axis=0)[:TILES_OUT, :NBOX]
     arrived(peaks_in.at[pl.ds(0, BANDS - 1)], peak_send)
+
+
+def finish(dm_ref, peak_ref, dm_out, peak_out, sem):
+    copies = [
+        pltpu.make_async_copy(dm_ref, dm_out, sem.at[0]),
+        pltpu.make_async_copy(peak_ref, peak_out, sem.at[1]),
+    ]
+    for copy in copies:
+        copy.start()
+    for copy in copies:
+        copy.wait()
 
 
 def local(intensity, chan_shift, sub_shift, widths):
@@ -296,6 +319,7 @@
             pltpu.VMEM((8, LANES), F32),
             pltpu.VMEM((BANDS, 8, LANES), F32),
             pltpu.SemaphoreType.DMA((5,)),
+            pltpu.SemaphoreType.REGULAR,
             pltpu.SemaphoreType.DMA((HALVES,)),
             pltpu.SemaphoreType.DMA((HALVES, 2)),
             pltpu.SemaphoreType.DMA((HALVES,)),
@@ -308,6 +332,18 @@
         ),
         cost_estimate=pl.CostEstimate(flops=4_000_000_000, bytes_accessed=2_000_000, transcendentals=0),
     )(*operands)
+    hbm = pl.BlockSpec(memory_space=pltpu.HBM)
+    dm, peak = pl.pallas_call(
+        finish,
+        out_shape=(
+            jax.ShapeDtypeStruct((OWN, TILES_OUT * LANES), BF16),
+            jax.ShapeDtypeStruct((TILES_OUT, NBOX), F32),
+        ),
+        in_specs=[vmem, vmem],
+        out_specs=(hbm, hbm),
+        scratch_shapes=[pltpu.SemaphoreType.DMA((2,))],
+        compiler_params=pltpu.CompilerParams(vmem_limit_bytes=16 << 20),
+    )(dm, peak)
     return dm.reshape(OWN, 1, TILES_OUT * LANES), peak.T.reshape(1, NBOX, TILES_OUT)
 
 

time: 60.6 us -> 59.8 us (0.987)
  local copies, waits for them, and re-layouts: 1.21 us -> 0 us
    unnamed x2 -> x0, local copies, waits for them, and re-layouts: 1.21 us -> none
    pallas_call x0 -> x1, Pallas kernels: none -> 0.65 us  [local(): pl.pallas_call(finish, out_shape=(jax.ShapeDtypeStruct((OWN, TILES_OUT *...]
where the time goes in v4:
time: 59.8 us; the launch traced here: 59.7 us
  Pallas kernels  59 us (99%)
  between operations  0.64 us (1%)
    pallas_call x1, Pallas kernels, local(): pl.pallas_call(kernel, out_shape=(jax.ShapeDtypeStruct((OWN, TILES_OUT *...  58.4 us

profile of v4, /device:TPU:1, one launch (start us, length us, event | category | flops | bytes accessed | tf_op | source)
XLA Modules:
  0.0 59.7 jit_solution(7970496636843064764)
XLA Ops:
  0.6 58.4 %shard_map.59 = (bf16[64,512]{1,0:T(8,128)(2,1)S(1)}, f32[4,16]{1,0:T(4,128)S(1)}) custom-call(bf16[40,32,256]{2,1,0:T(8,128)(2,1)} %x_hbm.1, s32[32,256]{1,0:T(8,128)} %chan_hbm.1, s32[1024,256]{1,0:T(8,128)} %shift_hbm.1, s32[16]{0:T(128)} %width_hbm.1), custom_call_target="tpu_custom_call" | custom-call | flops 4000000000 | bytes 2000000 | tf_op jit(solution)/shard_map/pallas_call | solution.py:296
  59.0 0.7 %shard_map.60 = (bf16[64,512]{1,0:T(8,128)(2,1)}, f32[4,16]{1,0:T(4,128)}) custom-call(bf16[64,512]{1,0:T(8,128)(2,1)S(1)} %get-tuple-element.6.dm_ref, f32[4,16]{1,0:T(4,128)S(1)} %get-tuple-element.7.peak_ref), custom_call_target="tpu_custom_call" | custom-call | tf_op jit(solution)/shard_map/pallas_call | solution.py:336

commit v5 on v4

--- a/solution.py
+++ b/solution.py
@@ -12,6 +12,7 @@
 SAMPLES = 40
 BEAMS = 32
 RING = 16
+AHEAD = 1
 BANDS = 16
 HALVES = 2
 GROUPS = 32
@@ -119,14 +120,24 @@
 
     def send_beams(h, own):
         def send(i, _):
-            skip = lax.rem(RING - place, RING)
-            step = i if h == 0 else jnp.where(i == own, skip, jnp.where(i <= skip, i - 1, i))
-            if h == 1 and own:
-                step = jnp.where(place == 0, i, step)
-            send_block(h, own, step)
+            there = lax.rem(place + i, RING)
+
+            @pl.when((h == 0) | (there >= AHEAD))
+            def _():
+                send_block(h, own, i)
+
             return 0
 
         lax.fori_loop(own, RING, send, 0)
+
+    def send_ahead(there, _):
+        send_block(1, 0, there - place)
+
+        @pl.when(there != place)
+        def _():
+            send_block(1, 1, there - place)
+
+        return 0
 
     send_beams(0, 1)
     gather(1)
@@ -136,6 +147,7 @@
         pl.semaphore_wait(ready, 1)
 
     send_beams(0, 0)
+    lax.fori_loop(0, AHEAD, send_ahead, 0)
     send_beams(1, 0)
 
     loads[2].wait()
@@ -231,8 +243,9 @@
                         ]
 
     subseries(0, 1, False)
-    send_beams(1, 1)
+    pl.when(place > 0)(lambda: send_beams(1, 1))
     subseries(0, 0, True)
+    pl.when(place == 0)(lambda: send_beams(1, 1))
     trials(0)
     subseries(1, 0, False)
     subseries(1, 1, True)

time: 59.8 us -> 59.6 us (level)
  no operation moved by 1% of the time
where the time goes in v5:
time: 59.6 us; the launch traced here: 59.4 us
  Pallas kernels  58.8 us (99%)
  between operations  0.64 us (1%)
    pallas_call x1, Pallas kernels, local(): pl.pallas_call(kernel, out_shape=(jax.ShapeDtypeStruct((OWN, TILES_OUT *...  58.2 us

profile of v5, /device:TPU:1, one launch (start us, length us, event | category | flops | bytes accessed | tf_op | source)
XLA Modules:
  0.0 59.4 jit_solution(12765588937790717856)
XLA Ops:
  0.6 58.2 %shard_map.59 = (bf16[64,512]{1,0:T(8,128)(2,1)S(1)}, f32[4,16]{1,0:T(4,128)S(1)}) custom-call(bf16[40,32,256]{2,1,0:T(8,128)(2,1)} %x_hbm.1, s32[32,256]{1,0:T(8,128)} %chan_hbm.1, s32[1024,256]{1,0:T(8,128)} %shift_hbm.1, s32[16]{0:T(128)} %width_hbm.1), custom_call_target="tpu_custom_call" | custom-call | flops 4000000000 | bytes 2000000 | tf_op jit(solution)/shard_map/pallas_call | solution.py:309
  58.8 0.7 %shard_map.60 = (bf16[64,512]{1,0:T(8,128)(2,1)}, f32[4,16]{1,0:T(4,128)}) custom-call(bf16[64,512]{1,0:T(8,128)(2,1)S(1)} %get-tuple-element.6.dm_ref, f32[4,16]{1,0:T(4,128)S(1)} %get-tuple-element.7.peak_ref), custom_call_target="tpu_custom_call" | custom-call | tf_op jit(solution)/shard_map/pallas_call | solution.py:349
